TPU v7x, 32 devices: a whole 2x2x4 slice. The times are simulated.
32 devices in a mesh: rep: 4 (over x, core), own: 8 (over z, y).
Axes of the slice: x: 2, y: 2, z: 4, core: 2. Of those that a mesh axis runs over, the one named last changes fastest.
Arguments:
- layer_input: float32 [8192, 1024], P(('rep', 'own')), may hold values from -6 to 6
- output_grad: float32 [8192, 1024], P(('rep', 'own')), may hold values from -12 to 12
- lengths: int32 [32, 3], P(('rep', 'own')), may hold values from 1 to 224, 256 in all within a row
- attention_gain: float32 [1024], replicated, may hold values from 0.25 to 1.75
- feed_gain: float32 [1024], replicated, may hold values from 0.25 to 1.75
- query_gain: float32 [128], replicated, may hold values from 0.25 to 1.75
- key_gain: float32 [128], replicated, may hold values from 0.25 to 1.75
- query_weight: float32 [1024, 2048], P('own'), may hold values from -0.1875 to 0.1875
- key_weight: float32 [1024, 1024], P('own'), may hold values from -0.1875 to 0.1875
- value_weight: float32 [1024, 1024], P('own'), may hold values from -0.1875 to 0.1875
- out_weight: float32 [2048, 1024], P('own'), may hold values from -0.75 to 0.75
- gate_weight: float32 [1024, 3072], P('own'), may hold values from -0.1875 to 0.1875
- up_weight: float32 [1024, 3072], P('own'), may hold values from -0.1875 to 0.1875
- down_weight: float32 [3072, 1024], P('own'), may hold values from -0.109375 to 0.109375
- query_moment: float32 [1024, 2048], P('own'), may hold values from -320 to 320
- key_moment: float32 [1024, 1024], P('own'), may hold values from -320 to 320
- value_moment: float32 [1024, 1024], P('own'), may hold values from -320 to 320
- out_moment: float32 [2048, 1024], P('own'), may hold values from -112 to 112
- gate_moment: float32 [1024, 3072], P('own'), may hold values from -224 to 224
- up_moment: float32 [1024, 3072], P('own'), may hold values from -224 to 224
- down_moment: float32 [3072, 1024], P('own'), may hold values from -448 to 448
Outputs:
- block_output: float32 [8192, 1024], P(('rep', 'own'))
- input_grad: float32 [8192, 1024], P(('rep', 'own'))
- norm_grads: float32 [2, 1024], replicated
- head_grads: float32 [2, 128], replicated
- query_updated: float32 [1024, 2048], P('own')
- key_updated: float32 [1024, 1024], P('own')
- value_updated: float32 [1024, 1024], P('own')
- out_updated: float32 [2048, 1024], P('own')
- gate_updated: float32 [1024, 3072], P('own')
- up_updated: float32 [1024, 3072], P('own')
- down_updated: float32 [3072, 1024], P('own')
- query_momentum: float32 [1024, 2048], P('own')
- key_momentum: float32 [1024, 1024], P('own')
- value_momentum: float32 [1024, 1024], P('own')
- out_momentum: float32 [2048, 1024], P('own')
- gate_momentum: float32 [1024, 3072], P('own')
- up_momentum: float32 [1024, 3072], P('own')
- down_momentum: float32 [3072, 1024], P('own')
Inputs may be any that keep to these rules, and one draw needn't show every extreme that they name: Row d lists in order the lengths of the 3 sequences that fill device d's 256 rows; each row sums to 256 and its longest is 224.
All inputs are finite; a program needn't handle non-finite values.
Results may differ from a plain program's by a relative error of at most 0.029.
Values may be sent and summed in bfloat16 or wider, within the bound.
A program may use at most 448 MiB of HBM per device.

v0:
```python
import functools

import jax
import jax.numpy as jnp
from jax import lax
from jax.experimental import pallas as pl
from jax.experimental.pallas import tpu as pltpu
from jax.sharding import PartitionSpec as P

HEADS = 16
KV_HEADS = 8
HEAD_DIM = 128
NS_STEPS = 5

EPSILON = 1e-06
ROPE_BASE = 1000000.0
MOMENTUM = 0.95
LEARN_RATE = 0.8
WEIGHT_DECAY = 0.01
NEWTON_A = 3.4445
NEWTON_B = -4.775
NEWTON_C = 2.0315

BF16 = jnp.bfloat16
F32 = jnp.float32
MESH = pl.DeviceIdType.MESH
ANY = pl.BlockSpec(memory_space=pltpu.HBM)

QKV, OUT, GU, DOWN = range(4)


def segments(lengths, row_count):
    seq_ends = jnp.cumsum(lengths)
    seq_starts = seq_ends - lengths
    row_ids = jnp.arange(row_count, dtype=jnp.int32)
    segment_ids = jnp.sum((row_ids[:, None] >= seq_ends[None, :]).astype(jnp.int32), 1)
    slot_ids = jnp.arange(lengths.shape[0], dtype=jnp.int32)
    row_starts = jnp.sum(
        jnp.where(segment_ids[:, None] == slot_ids[None, :], seq_starts[None, :], 0), 1
    )
    return (segment_ids, row_ids - row_starts)


def rope_tables(positions):
    inverse = ROPE_BASE ** (-jnp.arange(0, HEAD_DIM, 2, dtype=jnp.float32) / HEAD_DIM)
    angles = positions.astype(jnp.float32)[:, None] * inverse[None, :]
    return (jnp.cos(angles)[:, None, :], jnp.sin(angles)[:, None, :])


class Place:
    def __init__(self, n):
        self.n = n
        self.rep = lax.axis_index("rep")
        self.own = lax.axis_index("own")
        self.x = self.rep // 2
        self.core = self.rep % 2
        odd, pair = self.own % 2, self.own // 2
        self.ring = pair * (1 - odd) + odd * (n - 1 - pair)

    def own_at(self, ring):
        odd = ring // (self.n // 2)
        return 2 * (ring * (1 - odd) + odd * (self.n - 1 - ring)) + odd

    def shard(self, distance):
        return self.own_at(lax.rem(self.ring + distance + self.n, self.n))

    def ring_neighbour(self, way):
        return (self.rep, self.shard(way))

    @property
    def core_partner(self):
        return (self.x * 2 + 1 - self.core, self.own)

    @property
    def x_partner(self):
        return ((1 - self.x) * 2 + self.core, self.own)


def greet(devices):
    barrier = pltpu.get_barrier_semaphore()
    for device in devices:
        pl.semaphore_signal(barrier, inc=1, device_id=device, device_id_type=MESH)
    pl.semaphore_wait(barrier, len(devices))


class Several:
    def __init__(self, whole, copies):
        self.whole = whole
        self.copies = copies

    def start(self):
        for copy in self.copies:
            copy().start()

    def wait_send(self):
        self.whole().wait_send()

    def wait_recv(self):
        self.whole().wait_recv()


def remote(src, dst, send, recv, device):
    return pltpu.make_async_remote_copy(
        src_ref=src, dst_ref=dst, send_sem=send, recv_sem=recv, device_id=device, device_id_type=MESH
    )


def hops(n, way, kind):
    return n // 2 if (way == 0) == (kind == 0) else n // 2 - 1


SPREADS = ((QKV, True), (OUT, False), (GU, True), (DOWN, False))


def layer_kernel(n, tokens, unit, *refs):
    (
        x_ref, back_ref, table_ref, attention_gain, feed_gain, query_gain, key_gain,
    ) = refs[:7]
    shards = refs[7:11]
    output, input_grad, grad_attention, grad_feed, grad_query_gain, grad_key_gain = refs[11:17]
    grads = refs[17:21]
    (
        w_qkv, w_out, w_gu, w_down, normed, raw, low, probs, context, hidden, out_low, attended,
        grad_context, activated, gu_back, part, sent, got, middle, tables, stage, turned_left, gain_sums,
        local, ring_send, ring_recv, x_send, x_recv, swap_send, swap_recv, stage_sem,
    ) = refs[21:]
    weights = (w_qkv, w_out, w_gu, w_down)
    place = Place(n)
    top = n // 2
    cw, ccw = place.ring_neighbour(1), place.ring_neighbour(-1)
    ways = ((1, cw), (-1, ccw))
    greet([cw, ccw, place.core_partner, place.x_partner])
    both = 2 * tokens
    mine = pl.multiple_of(place.core * tokens, tokens)
    theirs = pl.multiple_of((1 - place.core) * tokens, tokens)
    my_rows, their_rows = pl.ds(mine, tokens), pl.ds(theirs, tokens)
    chunk = unit // 2
    ff = 3 * unit // 2
    few = 32
    base = unit // n
    heads = unit // HEAD_DIM
    kv_heads = heads // 2
    scale = HEAD_DIM ** (-0.5)

    def holds(which, own_index, act):
        if SPREADS[which][1]:
            act()
        else:
            pl.when(own_index // top == place.core)(act)

    def region(which, own_index, x):
        array, split = SPREADS[which]
        height = shards[which].shape[0]
        if split:
            width = weights[which].shape[1] // 2
            start = pl.multiple_of(own_index * height, height)
            return weights[which].at[pl.ds(start, height), pl.ds(pl.multiple_of(x * width, width), width)]
        start = pl.multiple_of(lax.rem(own_index, top) * height, height)
        return weights[which].at[pl.ds(start, height)]

    def own_copy(which):
        height = shards[which].shape[0]
        index = place.own if SPREADS[which][1] else lax.rem(place.own, top)
        start = pl.multiple_of(index * height, height)
        return pltpu.make_async_copy(
            shards[which], weights[which].at[pl.ds(start, height)], local.at[which]
        )

    def reach(which, way):
        return hops(n, way, 0 if SPREADS[which][1] else 1)

    def ring_copy(which, way, hop, act):
        step, target = ways[way]
        own_index = place.shard(-step * (hop if act == "wait_recv" else hop - 1))
        spot = region(which, own_index, place.x)
        index = (which * 2 + way) * top + hop - 1

        def do():
            copy = remote(spot, spot, ring_send.at[index], ring_recv.at[index], target)
            getattr(copy, act)()

        holds(which, own_index, do)

    def send_on(which, way, hop):
        ring_copy(which, way, hop, "start")

    def x_copy(which, way, hop, x):
        spot = region(which, place.shard(-ways[way][0] * hop), x)
        index = (which // 2 * 2 + way) * top + hop - 1
        return remote(spot, spot, x_send.at[index], x_recv.at[index], place.x_partner)

    def serve(which, hop):
        for way in range(2):
            if hop > reach(which, way):
                continue
            ring_copy(which, way, hop, "wait_recv")
            if hop < reach(which, way):
                send_on(which, way, hop + 1)
            if SPREADS[which][1]:
                x_copy(which, way, hop, place.x).start()

    def begin(which):
        def act():
            own_copy(which).wait()

        holds(which, place.own, act)
        for way in range(2):
            if reach(which, way) > 0:
                send_on(which, way, 1)

    def take_x(which):
        for way in range(2):
            for hop in range(1, reach(which, way) + 1):
                x_copy(which, way, hop, 1 - place.x).wait_recv()

    def swap(index, src, dst):
        return remote(src, dst, swap_send.at[index], swap_recv.at[index], place.core_partner)

    def rows_swap(index, ref):
        return swap(index, ref.at[my_rows], ref.at[my_rows])

    def part_swap(index, slot):
        return swap(index, sent.at[slot], got.at[slot])

    def loop(size, step, act):
        def body(k, carry):
            act(pl.multiple_of(k * step, step))
            return carry

        lax.fori_loop(0, size // step, body, 0)

    def normalize(source, gain, target):
        def act(k):
            value = source[pl.ds(k, few), :]
            value = value * lax.rsqrt(jnp.mean(value * value, -1, keepdims=True) + EPSILON)
            target[pl.ds(pl.multiple_of(mine + k, few), few), :] = (value * gain[...]).astype(BF16)

        loop(tokens, few, act)

    def normalize_back(k, source, gain, grad):
        value = source[pl.ds(k, few), :]
        inverse = lax.rsqrt(jnp.mean(value * value, -1, keepdims=True) + EPSILON)
        unscaled = value * inverse
        inner = grad * gain[...]
        back = inverse * (inner - unscaled * jnp.mean(inner * unscaled, -1, keepdims=True))
        return back, jnp.sum((grad * unscaled).reshape(few // 8, 8, unit), 0)

    def dot(left, right, across):
        return lax.dot_general(left, right, ((across[0], across[1]), ((), ())), preferred_element_type=F32)

    NN, NT, TN = ((1,), (0,)), ((1,), (1,)), ((0,), (0,))

    def partial_product(index, slot, left, right, across):
        part[...] = dot(left[...], right[...], across)

        def pack(k):
            sent[slot, pl.ds(k, few), :] = part[
                pl.ds(pl.multiple_of(theirs + k, few), few), :
            ].astype(BF16)

        loop(tokens, few, pack)
        part_swap(index, slot).start()

    def whole_rows(k, slot):
        own = part[pl.ds(pl.multiple_of(mine + k, few), few), :]
        return own + got[slot, pl.ds(k, few), :].astype(F32)

    def weight_grad(which, left, right):
        columns = right.shape[1] // unit

        def by_rows(r, carry):
            row = pl.multiple_of(r * chunk, chunk)
            turned_left[...] = left[:, pl.ds(row, chunk)].T

            def by_columns(c, carry):
                column = pl.multiple_of(c * unit, unit)
                index = r * columns + c
                slot = lax.rem(index, 2)

                @pl.when(index >= 2)
                def _():
                    stage_copy(which, slot, row, column, chunk, unit).wait()

                value = dot(turned_left[...], right[:, pl.ds(column, unit)], NN)
                stage[slot] = value.astype(BF16)
                stage_copy(which, slot, row, column, chunk, unit).start()
                return carry

            lax.fori_loop(0, columns, by_columns, 0)
            return carry

        lax.fori_loop(0, left.shape[1] // chunk, by_rows, 0)
        for slot in range(2):
            stage_copy(which, slot, 0, 0, chunk, unit).wait()

    def stage_copy(which, slot, row, column, height, width):
        return pltpu.make_async_copy(
            stage.at[slot], grads[which].at[pl.ds(row, height), pl.ds(column, width)],
            stage_sem.at[slot],
        )

    for which in range(4):
        holds(which, place.own, lambda: own_copy(which).start())
    tables[my_rows, :] = table_ref[...]
    normalize(x_ref, attention_gain, normed)
    rows_swap(0, normed).start()
    rows_swap(1, tables).start()
    begin(0)
    begin(1)

    def round_back(k):
        out_low[pl.ds(pl.multiple_of(mine + k, few), few), :] = back_ref[pl.ds(k, few), :].astype(BF16)

    loop(tokens, few, round_back)
    rows_swap(2, out_low).start()
    gain_sums[...] = jnp.zeros_like(gain_sums)

    late = [(1, top)] if top < 3 else [(1, h) for h in range(3, top + 1)]
    serve(0, 1)
    serve(1, 1)
    begin(2)
    for hop in range(2, top + 1):
        serve(0, hop)
        if (1, hop) not in late:
            serve(1, hop)
        if hop == 2:
            serve(2, 1)
    take_x(0)
    begin(3)
    pending = late + [(2, h) for h in range(2, top)] + [(3, 1), (2, top)]
    pending += [(3, h) for h in range(2, top + 1)]
    for name in (0, 1):
        rows_swap(name, (normed, tables)[name]).wait_recv()

    raw[:, pl.ds(0, unit)] = dot(normed[...], w_qkv[:, pl.ds(0, unit)], NN)
    keys_values = dot(normed[...], w_qkv[:, pl.ds(unit, unit)], NN)
    raw[:, pl.ds(unit, chunk)] = keys_values[:, :chunk]
    low[:, pl.ds(unit + chunk, chunk)] = keys_values[:, chunk:].astype(BF16)
    serve(*pending.pop(0))

    def turned(value, rows):
        return value * tables[rows, pl.ds(0, HEAD_DIM)] + pltpu.roll(
            value, HEAD_DIM // 2, 1
        ) * tables[rows, pl.ds(HEAD_DIM, HEAD_DIM)]

    def turned_back(value, rows):
        return value * tables[rows, pl.ds(0, HEAD_DIM)] - pltpu.roll(
            value, HEAD_DIM // 2, 1
        ) * tables[rows, pl.ds(HEAD_DIM, HEAD_DIM)]

    def head_norm(first, count, gain):
        def act(k):
            for half in range(2):
                rows = pl.ds(half * tokens, tokens)
                columns = pl.ds(pl.multiple_of(first + k, HEAD_DIM), HEAD_DIM)
                value = raw[rows, columns]
                inverse = lax.rsqrt(jnp.mean(value * value, -1, keepdims=True) + EPSILON)
                low[rows, columns] = turned(value * inverse * gain[...], rows).astype(BF16)

        loop(count * HEAD_DIM, HEAD_DIM, act)

    head_norm(0, heads, query_gain)
    if pending:
        serve(*pending.pop(0))
    head_norm(unit, kv_heads, key_gain)

    def spans(k, half):
        queries = [pl.ds(pl.multiple_of((2 * k + g) * HEAD_DIM, HEAD_DIM), HEAD_DIM) for g in range(2)]
        keys = pl.ds(pl.multiple_of(unit + k * HEAD_DIM, HEAD_DIM), HEAD_DIM)
        values = pl.ds(pl.multiple_of(unit + unit // 2 + k * HEAD_DIM, HEAD_DIM), HEAD_DIM)
        return queries, keys, values, pl.ds(half * tokens, tokens)

    def stacked(ref, rows, columns):
        return jnp.concatenate([ref[rows, columns[0]], ref[rows, columns[1]]], 0)

    def attend(k, half):
        queries, keys, values, rows = spans(k, half)
        row_id = lax.broadcasted_iota(jnp.int32, (tokens, tokens), 0)
        column_id = lax.broadcasted_iota(jnp.int32, (tokens, tokens), 1)
        start = tables[rows, pl.ds(2 * HEAD_DIM, HEAD_DIM)][:, :1]
        allowed = (column_id <= row_id) & (column_id.astype(F32) >= start)
        masks = jnp.where(allowed, 0.0, -1e30)
        scores = dot(stacked(low, rows, queries), low[rows, keys], NT) * scale
        scores = scores + jnp.concatenate([masks, masks], 0)
        exponent = jnp.exp(scores - jnp.max(scores, -1, keepdims=True))
        value = exponent / jnp.sum(exponent, -1, keepdims=True)
        probs[k * 2 + half] = value
        result = dot(value.astype(BF16), low[rows, values], NN).astype(BF16)
        for g in range(2):
            context[rows, queries[g]] = result[g * tokens : (g + 1) * tokens]

    for k in range(kv_heads):
        for half in range(2):
            attend(k, half)
        if pending and k % 2 == 0:
            serve(*pending.pop(0))

    while pending and pending[0][0] == 1:
        serve(*pending.pop(0))
    partial_product(3, 0, context, w_out, NN)
    if pending and pending[0][0] == 2:
        serve(*pending.pop(0))
    part_swap(3, 0).wait_recv()

    def add_middle(k):
        middle[pl.ds(k, few), :] = x_ref[pl.ds(k, few), :] + whole_rows(k, 0)

    loop(tokens, few, add_middle)
    normalize(middle, feed_gain, hidden)
    rows_swap(4, hidden).start()
    while pending:
        serve(*pending.pop(0))
    take_x(2)
    rows_swap(4, hidden).wait_recv()
    rows_swap(2, out_low).wait_recv()

    def feed(k):
        span = pl.ds(k, chunk)
        pair = pl.ds(pl.multiple_of(2 * k, unit), unit)
        gate_up = dot(hidden[...], w_gu[:, pair], NN)
        gate, up = gate_up[:, :chunk], gate_up[:, chunk:]
        grad = dot(out_low[...], w_down[span, :], NT)
        sigmoid = 1.0 / (1.0 + jnp.exp(-gate))
        swish = gate * sigmoid
        activated[:, span] = (swish * up).astype(BF16)
        gu_back[:, pl.ds(pl.multiple_of(2 * k, chunk), chunk)] = (
            grad * up * (sigmoid + swish * (1.0 - sigmoid))
        ).astype(BF16)
        gu_back[:, pl.ds(pl.multiple_of(2 * k + chunk, chunk), chunk)] = (grad * swish).astype(BF16)

    loop(ff, chunk, feed)
    part_swap(3, 0).wait_send()
    partial_product(6, 0, gu_back, w_gu, NT)
    weight_grad(3, activated, out_low)
    part_swap(6, 0).wait_recv()

    def middle_back(k):
        back, gain_part = normalize_back(k, middle, feed_gain, whole_rows(k, 0))
        back = back_ref[pl.ds(k, few), :] + back
        input_grad[pl.ds(k, few), :] = back
        attended[pl.ds(pl.multiple_of(mine + k, few), few), :] = back.astype(BF16)
        gain_sums[1] += gain_part

    loop(tokens, few, middle_back)
    rows_swap(7, attended).start()
    partial_product(5, 1, activated, w_down, NN)
    weight_grad(2, hidden, gu_back)
    part_swap(5, 1).wait_recv()

    def add_output(k):
        output[pl.ds(k, few), :] = middle[pl.ds(k, few), :] + whole_rows(k, 1)

    loop(tokens, few, add_output)
    rows_swap(7, attended).wait_recv()

    grad_context[...] = dot(attended[...], w_out[...], NT).astype(BF16)
    weight_grad(1, context, attended)

    def head_back(rows, columns, gain, grad, index):
        value = raw[rows, columns]
        inverse = lax.rsqrt(jnp.mean(value * value, -1, keepdims=True) + EPSILON)
        unscaled = value * inverse
        grad = turned_back(grad, rows)
        gain_sums[index, :, pl.ds(0, HEAD_DIM)] += jnp.sum(
            (grad * unscaled).reshape(tokens // 8, 8, HEAD_DIM), 0
        )
        inner = grad * gain[...]
        back = inverse * (inner - unscaled * jnp.mean(inner * unscaled, -1, keepdims=True))
        low[rows, columns] = back.astype(BF16)

    def attend_back(k, half):
        queries, keys, values, rows = spans(k, half)
        prob = probs[k * 2 + half]
        above = stacked(grad_context, rows, queries)
        query_pair = stacked(low, rows, queries)
        grad_values = dot(prob.astype(BF16), above, TN)
        grad_probs = dot(above, low[rows, values], NT)
        grad_scores = prob * (grad_probs - jnp.sum(prob * grad_probs, -1, keepdims=True))
        grad_scores = grad_scores.astype(BF16)
        grad_queries = dot(grad_scores, low[rows, keys], NN) * scale
        grad_keys = dot(grad_scores, query_pair, TN) * scale
        for g in range(2):
            head_back(rows, queries[g], query_gain, grad_queries[g * tokens : (g + 1) * tokens], 2)
        head_back(rows, keys, key_gain, grad_keys, 3)
        low[rows, values] = grad_values.astype(BF16)

    def back_body(k, carry):
        for half in range(2):
            attend_back(k, half)
        return carry

    lax.fori_loop(0, kv_heads, back_body, 0)

    part_swap(6, 0).wait_send()
    partial_product(8, 0, low, w_qkv, NT)
    weight_grad(0, normed, low)
    part_swap(8, 0).wait_recv()

    def input_back(k):
        back, gain_part = normalize_back(k, x_ref, attention_gain, whole_rows(k, 0))
        input_grad[pl.ds(k, few), :] += back
        gain_sums[0] += gain_part

    loop(tokens, few, input_back)
    grad_attention[...] = jnp.sum(gain_sums[0], 0, keepdims=True)
    grad_feed[...] = jnp.sum(gain_sums[1], 0, keepdims=True)
    grad_query_gain[...] = jnp.sum(gain_sums[2, :, pl.ds(0, HEAD_DIM)], 0, keepdims=True)
    grad_key_gain[...] = jnp.sum(gain_sums[3, :, pl.ds(0, HEAD_DIM)], 0, keepdims=True)

    for index, ref in ((0, normed), (1, tables), (2, out_low), (4, hidden), (7, attended)):
        rows_swap(index, ref).wait_send()
    part_swap(5, 1).wait_send()
    part_swap(8, 0).wait_send()
    for which in range(4):
        for way in range(2):
            for hop in range(1, reach(which, way) + 1):
                ring_copy(which, way, hop, "wait_send")
                if SPREADS[which][1]:
                    x_copy(which, way, hop, place.x).wait_send()


def layer_pass(values, back, table, gains, shards, n):
    tokens, unit = values.shape
    top = n // 2
    dma = pltpu.SemaphoreType.DMA
    vmem = pltpu.VMEM
    both = 2 * tokens
    heads = unit // HEAD_DIM
    in_vmem = pl.BlockSpec(memory_space=pltpu.VMEM)
    row = lambda width: jax.ShapeDtypeStruct((1, width), F32)
    shapes = [(unit, 2 * unit), (unit, unit), (unit, 3 * unit), (3 * unit // 2, unit)]
    results = pl.pallas_call(
        functools.partial(layer_kernel, n, tokens, unit),
        out_shape=[jax.ShapeDtypeStruct((tokens, unit), F32)] * 2
        + [row(unit), row(unit), row(HEAD_DIM), row(HEAD_DIM)]
        + [jax.ShapeDtypeStruct(shape, BF16) for shape in shapes],
        in_specs=[in_vmem] * 7 + [ANY] * 4,
        out_specs=[in_vmem] * 6 + [ANY] * 4,
        scratch_shapes=[vmem(shape, BF16) for shape in shapes]
        + [
            vmem((both, unit), BF16),
            vmem((both, 3 * unit // 2), F32),
            vmem((both, 2 * unit), BF16),
            vmem((heads, both, tokens), F32),
            vmem((both, unit), BF16),
            vmem((both, unit), BF16),
            vmem((both, unit), BF16),
            vmem((both, unit), BF16),
            vmem((both, unit), BF16),
            vmem((both, 3 * unit // 2), BF16),
            vmem((both, 3 * unit), BF16),
            vmem((both, unit), F32),
            vmem((2, tokens, unit), BF16),
            vmem((2, tokens, unit), BF16),
            vmem((tokens, unit), F32),
            vmem((both, 3 * HEAD_DIM), F32),
            vmem((2, unit // 2, unit), BF16),
            vmem((unit // 2, both), BF16),
            vmem((4, 8, unit), F32),
            dma((4,)),
            dma((8 * top,)),
            dma((8 * top,)),
            dma((4 * top,)),
            dma((4 * top,)),
            dma((9,)),
            dma((9,)),
            dma((2,)),
        ],
        compiler_params=pltpu.CompilerParams(
            collective_id=0, has_side_effects=True, vmem_limit_bytes=56 * 2**20
        ),
    )(values, back, table, *gains, *shards)
    return results[:2], results[2:6], results[6:]


PHASES = ((DOWN, 3, False), (GU, 3, True), (OUT, 2, False), (QKV, 2, True))

OWNERS = (
    (3, 0, 1, False, 1, 2),
    (3, 1, 1, False, 1, 6),
    (3, 0, 2, False, 0, 2),
    (2, 0, 2, True, 1, 5),
    (1, 0, 3, False, 0, 5),
    (1, 0, 3, False, 1, 1),
    (0, 0, 3, True, 0, 1),
)
KEY, VALUE, QUERY, OUTM, GATE, UP, DOWNM = range(7)
RETURNS = (OUTM, KEY, VALUE, DOWNM, GATE, UP, QUERY)
TILE_SLOTS = 4
X_AHEAD = 4
LAND_AHEAD = 6


def summing_core(phase):
    return 0 if PHASES[phase][2] else 1


def stage_order(n, core):
    rings = ((1.0, 1.5), (4.0, 2.7), (13.0, 1.1), (26.6, 1.7))
    crossings = {1: (-6.0, 2.5), 3: (16.0, 1.5)}
    keys, needs = {}, {}
    for phase in range(4):
        first, step = rings[phase]
        for i in range(n):
            key = first + step * i * 8 / n
            if summing_core(phase) == core:
                keys["ring", phase, i] = key
                needs["ring", phase, i] = [("ring", phase, i - 1)] if i else []
                if phase in crossings:
                    needs["ring", phase, i].append(("x", phase, i))
            else:
                keys["land", phase, i] = key - 6.0
                needs["land", phase, i] = [("land", phase, i - 1)] if i else []
        if phase in crossings:
            first, step = crossings[phase]
            for i in range(n):
                keys["x", phase, i] = first + step * i * 8 / n
                needs["x", phase, i] = [("x", phase, i - 1)] if i else [("x", 1, n - 1)] * (phase == 3)
                if core == 0 and phase == 3:
                    needs["x", phase, i].append(("ring", 1, i))
        elif core == 1:
            keys["final", phase, 0] = {0: 16.0, 2: 27.0}[phase]
            needs["final", phase, 0] = [("ring", phase, n - 1)]
    left, found = sorted(keys, key=lambda stage: (keys[stage], stage)), []
    while left:
        stage = next(stage for stage in left if all(need in found for need in needs[stage]))
        left.remove(stage)
        found.append(stage)
    return found


class Rows:
    def __init__(self):
        self.next = 0

    def take(self, rows):
        start = self.next
        self.next += rows
        return start


def layout(n, unit):
    base = unit // n
    top = n // 2
    place = {}
    rows = (Rows(), Rows())
    place["high"] = [None, rows[1].take(3 * unit)]
    for name in ("grad", "ahead"):
        place[name] = [rows[summing_core(p)].take(PHASES[p][1] * base) for p in range(4)]
    for name in ("part", "other"):
        place[name] = [0 if split else rows[1].take(units * base) for _, units, split in PHASES]
    newton = Rows()
    newton.next = -(-rows[1].next // unit) * unit
    place["high"][0] = newton.take(3 * unit)
    place["poly"] = [newton.take(unit) for _ in range(2)]
    place["x_in"] = [rows[0].take(3 * base) for _ in range(n)]
    place["own"] = [[rows[core].take(3 * base) for _ in range(TILE_SLOTS)] for core in range(2)]
    place["ring"], place["far"] = [], []
    for phase, (_, units, _) in enumerate(PHASES):
        take = rows[summing_core(phase)].take
        place["ring"].append([[take(units * base) for _ in range(top)] for _ in range(2)])
        place["far"].append(take(units * base))
    return place, max(rows[0].next, rows[1].next, newton.next)


def update_kernel(n, unit, *refs):
    grads, moments, gains_in = refs[:4], refs[4:11], refs[11]
    outs, orths, lands, gains_out = refs[12:16], refs[16:20], refs[20:24], refs[24]
    (
        pool, exact, gram, squares, gain_mine, gain_core, gain_x, gain_all,
        land_send, land_recv, tile_sem, x_send, x_recv, x_free, ring_send, ring_recv, part_send, part_recv,
        moment_sem, grad_local, grad_send, grad_recv, in_send, in_recv, in_local,
        out_send, out_recv, pass_send, pass_recv, gain_send, gain_recv,
    ) = refs[25:]
    place = Place(n)
    base = unit // n
    top = n // 2
    at, _ = layout(n, unit)
    cw, ccw = place.ring_neighbour(1), place.ring_neighbour(-1)
    ways = ((1, cw), (-1, ccw))
    side = [(place.x * 2 + core, lax.rem(place.own + k, n)) for k in range(1, n) for core in range(2)]
    across = [((1 - place.x) * 2 + core, place.own) for core in range(2)]
    greet(side + [place.core_partner] + across)
    order = [top]
    for distance in range(top - 1, 0, -1):
        order += [distance, -distance]
    order.append(0)
    moment = exact
    height = [units * base for _, units, _ in PHASES]
    moment_at = [sum(height[:phase]) for phase in range(4)]
    owners = [
        (xs * 2 + 1, place.own_at(spot * n // 8)) for _, _, _, _, xs, spot in OWNERS
    ]
    here = place.rep * n + place.own
    is_owner = [here == rep * n + own for rep, own in owners]

    def rows(start, size):
        if isinstance(start, int):
            return pl.ds(start, size)
        return pl.ds(pl.multiple_of(start, size), size)

    def block(start, size):
        return pool.at[rows(start, size)]

    def pieces_of(phase, x):
        array, units, _ = PHASES[phase]
        half = unit // 2
        found = []
        for core in range(2):
            for b in range(units):
                if array == GU:
                    own_column = b * unit + x * half
                    column = x * 3 * unit + core * (3 * half) + b * half
                else:
                    own_column = x * units * half + b * half
                    column = x * 2 * unit + core * (unit - x * half) + b * (half + x * half)
                found.append((core, b, own_column, column))
        return found

    def columns(start):
        return pl.ds(pl.multiple_of(start, unit // 2), unit // 2)

    def in_block(start, core, b):
        return pool.at[pl.ds(start + b * base, base), pl.ds(core * (unit // 2), unit // 2)]

    def shard_rows(phase, own_index):
        if PHASES[phase][2]:
            return rows(own_index * base, base)
        return rows(lax.rem(own_index, top) * height[phase], height[phase])

    def landing(phase, own_index, act):
        if PHASES[phase][2]:
            act()
        else:
            pl.when(own_index // top != summing_core(phase))(act)

    def spread(source, target, size, send, recv, device):
        step = size

        def copy(k, count):
            return remote(block(source + k, count), block(target + k, count), send, recv, device)

        return Several(
            functools.partial(copy, 0, size),
            [functools.partial(copy, k, step) for k in range(0, size, step)],
        )

    def land_copy(phase, i, act):
        array, units, split = PHASES[phase]
        own_index = place.shard(order[i])
        span = shard_rows(phase, own_index)

        def copy(at_columns):
            return remote(
                grads[array].at[span, at_columns], lands[array].at[span, at_columns],
                land_send.at[phase * n + i], land_recv.at[phase * n + i], place.core_partner,
            )

        def do():
            if not split:
                getattr(copy(pl.ds(0, unit)), act)()
            elif act == "start":
                for core, _, column, _ in pieces_of(phase, place.x):
                    if core == 1:
                        copy(columns(column)).start()
            else:
                getattr(copy(pl.ds(0, units * unit // 2)), act)()

        landing(phase, own_index, do)

    def x_index(phase, i):
        return (phase // 2) * n + i

    def x_copies(phase, i, core, act):
        index = x_index(phase, i)
        array, units, _ = PHASES[phase]
        span = shard_rows(phase, place.shard(order[i]))
        target = at["x_in"][i]

        def copy(source, spot):
            return remote(
                source, spot, x_send.at[index], x_recv.at[core, index], ((1 - place.x) * 2, place.own)
            )

        if act == "start":
            for its_core, b, column, _ in pieces_of(phase, 1 - place.x):
                if its_core == core:
                    copy(grads[array].at[span, columns(column)], in_block(target, core, b)).start()
        else:
            spot = pool.at[pl.ds(target, height[phase]), pl.ds(core * (unit // 2), unit // 2)]
            getattr(copy(spot, spot), act)()

    def ring_copy(phase, way, distance, source, part):
        size = height[phase] // 2
        target = at["ring"][phase][way][distance - 1] + part * size
        index = ((phase * 2 + way) * top + distance - 1) * 2 + part
        return spread(
            source + part * size, target, size,
            ring_send.at[index], ring_recv.at[index], ways[way][1],
        )

    def ring_out(phase, distance, part):
        if distance == 0:
            return []
        if distance == top:
            return [ring_copy(phase, part, top, at["far"][phase], part)]
        way = 0 if distance > 0 else 1
        far = abs(distance)
        return [ring_copy(phase, way, far, at["ring"][phase][way][far], part)]

    def part_copy(phase):
        return spread(
            at["part"][phase], at["other"][phase], height[phase],
            part_send.at[phase // 2], part_recv.at[phase // 2], place.x_partner,
        )

    def gain_copy(src, dst, slot, device):
        return remote(src, dst, gain_send.at[slot], gain_recv.at[slot], device)

    def gain_core_copy():
        return gain_copy(gain_mine, gain_core, 0, place.core_partner)

    def gain_x_copy():
        return gain_copy(gain_core, gain_x, 1, place.x_partner)

    def gain_back_copy():
        return gain_copy(gain_mine, gain_x, 2, place.core_partner)

    def gain_ring(way, hop, distance):
        spot = gain_all.at[place.shard(distance)]
        return gain_copy(spot, spot, 3 + way * top + hop - 1, ways[way][1])

    def grad_place(phase, x):
        array = PHASES[phase][0]
        start = at["grad"][phase]
        if not PHASES[phase][2]:
            return [(outs[array], block(start, height[phase]))]
        return [
            (outs[array].at[:, columns(column)], in_block(start, core, b))
            for core, b, _, column in pieces_of(phase, x)
        ]

    def grad_span(phase, x):
        array, units, split = PHASES[phase]
        if not split:
            return outs[array]
        first = pl.multiple_of(x * units * unit, unit)
        return outs[array].at[:, pl.ds(first, units * unit)]

    def grad_sent(phase, to, device, x):
        span = grad_span(phase, x)
        return remote(span, span, grad_send.at[phase, to], grad_recv.at[phase, to], device)

    def matrix_rows(matrix, own_index):
        phase, first, units, tall, _, _ = OWNERS[matrix]
        if tall:
            return [(0, own_index * units * base, units * base)]
        return [
            ((first + k) * base, k * unit + own_index * base, base) for k in range(units)
        ]

    def matrix_span(matrix):
        phase, first, units, tall, xs, _ = OWNERS[matrix]
        array = PHASES[phase][0]
        if tall:
            return orths[array]
        start = (xs * PHASES[phase][1] + first) * unit
        return orths[array].at[:, pl.ds(start, units * unit)]

    def answer_parts(matrix, final, own_index):
        phase, first, units, tall, xs, _ = OWNERS[matrix]
        array = PHASES[phase][0]
        if tall:
            return [(block(final + own_index * units * base, units * base), orths[array])]
        return [
            (
                pool.at[
                    rows(final + (b - first) * unit + own_index * base, base),
                    pl.ds(core * (unit // 2), unit // 2),
                ],
                orths[array].at[:, columns(column)],
            )
            for core, b, _, column in pieces_of(phase, xs)
            if first <= b < first + units
        ]

    def handed(matrix, to, device):
        span = matrix_span(matrix)
        return remote(span, span, pass_send.at[matrix, to], pass_recv.at[matrix, to], device)

    def answered(matrix, target):
        span = matrix_span(matrix)
        return remote(
            span, span, out_send.at[target], out_recv.at[matrix], (place.x * 2, target)
        )

    def summed(pieces, size, store):
        step = 16
        steps = 4 if size % (4 * step) == 0 else 1

        def body(k, carry):
            for j in range(steps):
                shift = (k * steps + j) * step
                total = None
                for start in pieces:
                    value = pool[rows_at(start, shift, step), :].astype(F32)
                    total = value if total is None else total + value
                store(shift, step, total)
            return carry

        lax.fori_loop(0, size // (step * steps), body, 0)

    def rows_at(start, shift, step):
        return pl.ds(pl.multiple_of(start + shift, step), step)

    def keep(start):
        def store(shift, step, total):
            pool[rows_at(start, shift, step), :] = total.astype(BF16)

        return store

    def load_tile(phase, i, slot):
        array, _, split = PHASES[phase]
        own_index = place.shard(order[i])
        span = shard_rows(phase, own_index)
        summing = summing_core(phase)

        def load(source, target):
            pltpu.make_async_copy(source, target, tile_sem.at[slot]).start()

        if split:
            for core, b, column, _ in pieces_of(phase, place.x):
                load(
                    (grads, lands)[core][array].at[span, columns(column)],
                    in_block(at["own"][summing][slot], core, b),
                )
            return
        for core in range(2):

            @pl.when(own_index // top == core)
            def _():
                load(
                    (lands, grads)[core == summing][array].at[span],
                    block(at["own"][summing][slot], height[phase]),
                )

    def prefetch(rings, index):
        if index < len(rings):
            _, phase, i = rings[index]
            land_copy(phase, i, "wait_recv")
            load_tile(phase, i, index % TILE_SLOTS)

    def moment_copies(phase, act):
        array, units, split = PHASES[phase]
        if not split:
            act(moments[3 if array == OUT else 6], moment.at[pl.ds(moment_at[phase], height[phase])])
            return
        half = unit // 2
        for x in range(2):

            @pl.when(place.x == x)
            def _():
                for core, b, _, column in pieces_of(phase, x):
                    if array == GU:
                        source, first = 4 + x, x * 3 * unit
                    elif x == 0:
                        source, first = 0, 0
                    else:
                        source, first = 1 + b, (2 + b) * unit
                    act(
                        moments[source].at[:, pl.ds(column - first, half)],
                        moment.at[pl.ds(moment_at[phase] + b * base, base), pl.ds(core * half, half)],
                    )

    def load_moment(phase):
        moment_copies(
            phase, lambda src, dst: pltpu.make_async_copy(src, dst, moment_sem.at[phase]).start()
        )

    def finish(phase, pieces):
        span = moment.at[pl.ds(moment_at[phase], height[phase])]
        pltpu.make_async_copy(span, span, moment_sem.at[phase]).wait()

        def store(shift, step, total):
            pool[rows_at(at["grad"][phase], shift, step), :] = total.astype(BF16)
            ahead = (1.0 + MOMENTUM) * total + MOMENTUM**2 * moment[
                rows_at(moment_at[phase], shift, step), :
            ]
            pool[rows_at(at["ahead"][phase], shift, step), :] = ahead.astype(BF16)

        summed(pieces, height[phase], store)
        for matrix, (its_phase, _, _, _, xs, _) in enumerate(OWNERS):
            if its_phase != phase:
                continue

            def hand_in(local):
                for source, target, size in matrix_rows(matrix, place.own):
                    source = block(at["ahead"][phase] + source, size)
                    target = block(at["high"][1] + target, size)
                    if local:
                        pltpu.make_async_copy(source, target, in_local).start()
                    else:
                        remote(
                            source, target, in_send.at[matrix], in_recv.at[place.own], owners[matrix]
                        ).start()

            if summing_core(phase) == 0:
                pl.when(place.x == xs)(functools.partial(hand_in, False))
            else:
                pl.when(is_owner[matrix])(functools.partial(hand_in, True))
                pl.when((place.x == xs) & (here != owners[matrix][0] * n + owners[matrix][1]))(
                    functools.partial(hand_in, False)
                )

        for target, source in grad_place(phase, place.x):
            pltpu.make_async_copy(source, target, grad_local.at[phase]).start()
            remote(
                source, target, grad_send.at[phase, 0], grad_recv.at[phase, 0], place.core_partner
            ).start()
            if PHASES[phase][2]:
                remote(
                    source, target, grad_send.at[phase, 1], grad_recv.at[phase, 1], place.x_partner
                ).start()

    def settle(phase):
        span = block(at["grad"][phase], height[phase])
        pltpu.make_async_copy(span, span, grad_local.at[phase]).wait()
        remote(
            span, span, grad_send.at[phase, 0], grad_recv.at[phase, 0], place.core_partner
        ).wait_send()
        if PHASES[phase][2]:
            remote(
                span, span, grad_send.at[phase, 1], grad_recv.at[phase, 1], place.x_partner
            ).wait_send()
        for matrix, (its_phase, _, units, _, xs, _) in enumerate(OWNERS):
            if its_phase != phase:
                continue

            sends = place.x == xs
            if summing_core(phase) == 1:
                sends = sends & (here != owners[matrix][0] * n + owners[matrix][1])

            @pl.when(sends)
            def _():
                span = block(at["high"][1], units * base)
                remote(
                    span, span, in_send.at[matrix], in_recv.at[0], place.core_partner
                ).wait_send()

    def stage_x(phase, i, core):
        index = x_index(phase, i)
        if index >= X_AHEAD:
            before = index - X_AHEAD
            x_copies(1 if before < n else 3, before % n, core, "wait_send")
        if phase == 3:
            pl.semaphore_wait(x_free, 1)
        x_copies(phase, i, core, "start")

    def stage_ring(phase, i, slot):
        distance = order[i]
        start = at["own"][summing_core(phase)][slot]
        span = block(start, height[phase])
        pltpu.make_async_copy(span, span, tile_sem.at[slot]).wait()
        pieces = [start]
        if PHASES[phase][2]:
            for core in range(2):
                x_copies(phase, i, core, "wait_recv")
            pieces.append(at["x_in"][i])
        size = height[phase]
        mid = size // 2
        if distance == 0:
            for way in range(2):
                held = at["ring"][phase][way][0]
                for part in range(2):
                    ring_copy(phase, way, 1, held, part).wait_recv()
                pieces.append(held)
            if PHASES[phase][2]:
                finish(phase, pieces)
            else:
                summed(pieces, size, keep(at["part"][phase]))
                part_copy(phase).start()
        else:
            way = 0 if distance > 0 else 1
            far = abs(distance)
            held = at["far"][phase] if far == top else at["ring"][phase][way][far]
            for part in (1 - way, way):
                starts = [start + part * mid for start in pieces]
                if far + 1 < top or (far + 1 == top and part == way):
                    ring_copy(phase, way, far + 1, held, part).wait_recv()
                    starts.append(held + part * mid)
                summed(starts, mid, keep(held + part * mid))
                for copy in ring_out(phase, distance, part):
                    copy.start()
        if phase == 1:
            for device in across:
                pl.semaphore_signal(x_free, inc=1, device_id=device, device_id_type=MESH)

    def ring_sent(phase):
        for distance in order:
            for part in range(2):
                for copy in ring_out(phase, distance, part):
                    copy.wait_send()

    def run(core):
        stages = stage_order(n, core)
        rings = [stage for stage in stages if stage[0] == "ring"]
        landed = [stage for stage in stages if stage[0] == "land"]
        for phase in range(4):
            if summing_core(phase) == core:
                load_moment(phase)
        done, sent, hop = 0, 0, 0
        for index in range(LAND_AHEAD):
            land_copy(*landed[index][1:], "start")
        for index in range(TILE_SLOTS - 1):
            prefetch(rings, index)
        for kind, phase, i in stages:
            if kind == "x":
                stage_x(phase, i, core)
            elif kind == "land":
                land_copy(phase, i, "wait_send")
                if sent + LAND_AHEAD < len(landed):
                    land_copy(*landed[sent + LAND_AHEAD][1:], "start")
                sent += 1
            elif kind == "final":
                part_copy(phase).wait_recv()
                finish(phase, [at["part"][phase], at["other"][phase]])
            else:
                prefetch(rings, done + TILE_SLOTS - 1)
                stage_ring(phase, i, done % TILE_SLOTS)
                done += 1
                if core == 0 and hop <= top + 1:
                    gain_stage(hop)
                    hop += 1

    def settle_all(core):
        for phase, (_, _, split) in enumerate(PHASES):
            if summing_core(phase) == core:
                settle(phase)
                if not split:
                    part_copy(phase).wait_send()
        for index in range(2 * n - X_AHEAD, 2 * n):
            x_copies(1 if index < n else 3, index % n, core, "wait_send")

    def take_sums(core):
        for phase, (_, _, split) in enumerate(PHASES):
            if summing_core(phase) != core:
                grad_sent(phase, 0, place.core_partner, place.x).wait_recv()
                if split:
                    grad_sent(phase, 2, place.core_partner, 1 - place.x).wait_recv()

    def gain_stage(hop):
        if hop == 0:
            gain_core_copy().wait_recv()
            gain_core[...] = gain_mine[...] + gain_core[...]
            gain_x_copy().start()
            return
        if hop == 1:
            gain_x_copy().wait_recv()
            gain_all[place.own] = gain_core[...] + gain_x[...]
            for way in range(2):
                gain_ring(way, 1, 0).start()
        for way in range(2):
            if 1 < hop <= hops(n, way, 0) + 1:
                distance = -ways[way][0] * (hop - 1)
                gain_ring(way, hop - 1, distance).wait_recv()
                if hop <= hops(n, way, 0):
                    gain_ring(way, hop, distance).start()

    gain_mine[...] = gains_in[...]

    @pl.when(place.core == 0)
    def _():
        run(0)
        total = gain_all[0]
        for k in range(1, n):
            total = total + gain_all[k]
        gains_out[...] = total
        gain_mine[...] = total
        gain_back_copy().start()

        for phase in (1, 3):
            grad_sent(phase, 1, place.x_partner, 1 - place.x).wait_recv()
            grad_sent(phase, 2, place.core_partner, 1 - place.x).start()

        for matrix in RETURNS:
            xs = OWNERS[matrix][4]

            @pl.when(place.x == xs)
            def _():
                answered(matrix, place.own).wait_recv()
                handed(matrix, 0, place.x_partner).start()
                handed(matrix, 1, place.core_partner).start()

            @pl.when(place.x != xs)
            def _():
                handed(matrix, 0, place.x_partner).wait_recv()
                handed(matrix, 1, place.core_partner).start()

        for matrix, (phase, _, units, _, xs, _) in enumerate(OWNERS):
            handed(matrix, 1, place.core_partner).wait_send()

            @pl.when(place.x == xs)
            def _():
                handed(matrix, 0, place.x_partner).wait_send()

        take_sums(0)
        settle_all(0)
        for phase in (1, 3):
            ring_sent(phase)
            grad_sent(phase, 2, place.core_partner, 1 - place.x).wait_send()
        gain_x_copy().wait_send()
        gain_back_copy().wait_send()
        for way in range(2):
            for h in range(1, hops(n, way, 0) + 1):
                gain_ring(way, h, -ways[way][0] * (h - 1)).wait_send()

    @pl.when(place.core == 1)
    def _():
        gain_core_copy().start()
        run(1)
        for phase in (0, 2):
            ring_sent(phase)
        newton_part(n, unit, place, pool, exact, gram, squares, at, is_owner, in_recv, in_local)
        for matrix, (_, _, units, tall, _, _) in enumerate(OWNERS):

            @pl.when(is_owner[matrix])
            def _():
                final = at["high"][1 - NS_STEPS % 2 if tall else NS_STEPS % 2]

                def send(k, carry):
                    target = lax.rem(place.own + k, n)
                    for source, part in answer_parts(matrix, final, target):
                        remote(
                            source, part, out_send.at[target], out_recv.at[matrix],
                            (place.x * 2, target),
                        ).start()
                    return carry

                lax.fori_loop(0, n, send, 0)

                def sent(k, carry):
                    answered(matrix, lax.rem(place.own + k, n)).wait_send()
                    return carry

                lax.fori_loop(0, n, sent, 0)

        gain_core_copy().wait_send()
        gain_back_copy().wait_recv()
        gains_out[...] = gain_x[...]
        take_sums(1)
        settle_all(1)
        for matrix in RETURNS:
            handed(matrix, 1, place.core_partner).wait_recv()


def newton_part(n, unit, place, pool, exact, gram, squares, at, is_owner, in_recv, in_local):
    base = unit // n
    small = min(256, unit // 2)
    per = unit // small
    wide = unit // 2
    few = 32
    count, tall = 0, 0
    for mine, (_, _, units, lies_tall, _, _) in zip(is_owner, OWNERS):
        count = count + units * mine.astype(jnp.int32)
        tall = tall + int(lies_tall) * mine.astype(jnp.int32)
    high, poly = at["high"], at["poly"]

    def rows(start, size):
        return pl.ds(pl.multiple_of(start, size), size)

    for matrix, (phase, _, units, *_) in enumerate(OWNERS):

        @pl.when(is_owner[matrix])
        def _():
            span = pool.at[pl.ds(high[1], units * base)]
            inside = summing_core(phase) == 1
            if inside:
                pltpu.make_async_copy(span, span, in_local).wait()
            for k in range(1 if inside else 0, n):
                own_index = lax.rem(place.own + k, n)
                remote(
                    span, span, in_recv.at[own_index], in_recv.at[own_index], place.core_partner
                ).wait_recv()

    @pl.when(count > 0)
    def _():
        squares[...] = jnp.zeros_like(squares)

        def square(k, carry):
            part = pool[rows(high[1] + k * few, few), :].astype(F32)
            squares[...] += jnp.sum((part * part).reshape(few // 8, 8, unit), 0)
            return carry

        lax.fori_loop(0, count * (unit // few), square, 0)
        total = jnp.sum(jnp.sum(squares[...], 1, keepdims=True), 0, keepdims=True)
        inverse = 1.0 / (jnp.sqrt(total) + 1e-07)

        @pl.when(tall == 0)
        def _():
            def scale(k, carry):
                value = pool[rows(high[1] + k * few, few), :].astype(F32) * inverse
                exact[rows(k * few, few), :] = value
                pool[rows(high[0] + k * few, few), :] = value.astype(BF16)
                return carry

            lax.fori_loop(0, count * (unit // few), scale, 0)

        @pl.when(tall == 1)
        def _():
            def scale(k, carry):
                block, row = k // per, k % per
                for column in range(per):
                    part = pool[
                        rows(high[1] + k * small, small), pl.ds(column * small, small)
                    ].astype(F32)
                    value = (part * inverse).T
                    shift = block * unit + column * small
                    columns = rows(row * small, small)
                    exact[rows(shift, small), columns] = value
                    pool[rows(high[0] + shift, small), columns] = value.astype(BF16)
                return carry

            lax.fori_loop(0, count * per, scale, 0)

        def newton(step, carry):
            even = step % 2
            now = high[0] + even * (high[1] - high[0])
            later = high[1] - even * (high[1] - high[0])

            def keep_symmetric(to, chunk, value):
                pool[pl.ds(to, (chunk + 1) * wide), pl.ds(chunk * wide, wide)] = value.astype(BF16)
                if chunk == 1:
                    pool[pl.ds(to + wide, wide), pl.ds(0, wide)] = value[:wide].T.astype(BF16)

            for chunk in range(2):
                down = (chunk + 1) * wide

                def product(block):
                    left = pool[pl.ds(pl.multiple_of(now + block * unit, unit), down), :]
                    right = pool[rows(now + block * unit + chunk * wide, wide), :]
                    return lax.dot_general(
                        left, right, (((1,), (1,)), ((), ())), preferred_element_type=F32
                    )

                gram[:down, :] = product(0)

                def more(block, carry):
                    gram[:down, :] += product(block)
                    return carry

                lax.fori_loop(1, count, more, 0)
                keep_symmetric(poly[0], chunk, gram[:down, :])

            for chunk in range(2):
                down = (chunk + 1) * wide
                columns = pl.ds(chunk * wide, wide)
                squared = jnp.dot(
                    pool[pl.ds(poly[0], down), :], pool[pl.ds(poly[0], unit), columns],
                    preferred_element_type=F32,
                )
                plain = pool[pl.ds(poly[0], down), columns].astype(F32)
                keep_symmetric(poly[1], chunk, NEWTON_B * plain + NEWTON_C * squared)

            def advance(block, carry):
                for chunk in range(2):
                    columns = pl.ds(chunk * wide, wide)
                    value = NEWTON_A * exact[rows(block * unit, unit), columns] + jnp.dot(
                        pool[pl.ds(poly[1], unit), :],
                        pool[rows(now + block * unit, unit), columns],
                        preferred_element_type=F32,
                    )
                    exact[rows(block * unit, unit), columns] = value
                    pool[rows(later + block * unit, unit), columns] = value.astype(BF16)
                return carry

            lax.fori_loop(0, count, advance, 0)
            return carry

        lax.fori_loop(0, NS_STEPS, newton, 0)

        @pl.when(tall == 1)
        def _():
            free = high[1 - NS_STEPS % 2]
            factor = jnp.sqrt(jnp.full((1, 1), count, jnp.int32).astype(F32))

            def lay(k, carry):
                block, row = k // per, k % per
                for column in range(per):
                    columns = pl.ds(column * small, small)
                    part = exact[rows(k * small, small), columns]
                    pool[
                        rows(free + block * unit + column * small, small), rows(row * small, small)
                    ] = (part * factor).T.astype(BF16)
                return carry

            lax.fori_loop(0, count * per, lay, 0)


def update_all(grads, moments, gains, n, unit):
    top = n // 2
    dma = pltpu.SemaphoreType.DMA
    vmem = pltpu.VMEM
    _, pool_rows = layout(n, unit)
    shapes = [(unit // n, 4 * unit), (2 * unit // n, unit), (unit // n, 6 * unit), (3 * unit // n, unit)]
    own = [jax.ShapeDtypeStruct(shape, BF16) for shape in shapes]
    whole = [jax.ShapeDtypeStruct(grad.shape, BF16) for grad in grads]
    in_vmem = pl.BlockSpec(memory_space=pltpu.VMEM)
    results = pl.pallas_call(
        functools.partial(update_kernel, n, unit),
        out_shape=own + own + whole + [jax.ShapeDtypeStruct(gains.shape, F32)],
        in_specs=[ANY] * 11 + [in_vmem],
        out_specs=[ANY] * 12 + [in_vmem],
        scratch_shapes=[
            vmem((pool_rows, unit), BF16),
            vmem((3 * unit, unit), F32),
            vmem((unit, unit // 2), F32),
            vmem((8, unit), F32),
            vmem(gains.shape, F32),
            vmem(gains.shape, F32),
            vmem(gains.shape, F32),
            vmem((n,) + gains.shape, F32),
            dma((4 * n,)),
            dma((4 * n,)),
            dma((TILE_SLOTS,)),
            dma((2 * n,)),
            dma((2, 2 * n)),
            pltpu.SemaphoreType.REGULAR,
            dma((16 * top,)),
            dma((16 * top,)),
            dma((2,)),
            dma((2,)),
            dma((4,)),
            dma((4,)),
            dma((4, 3)),
            dma((4, 3)),
            dma((7,)),
            dma((n,)),
            dma,
            dma((n,)),
            dma((7,)),
            dma((7, 2)),
            dma((7, 2)),
            dma((3 + 2 * top,)),
            dma((3 + 2 * top,)),
        ],
        compiler_params=pltpu.CompilerParams(
            collective_id=1, has_side_effects=True, vmem_limit_bytes=56 * 2**20
        ),
    )(*grads, *moments, gains)
    return results[:4], results[4:8], results[12]


def apply_kernel(unit, *refs):
    weights, moments, sums, orths = refs[:7], refs[7:14], refs[14:18], refs[18:22]
    new_weights, new_moments = refs[22:29], refs[29:36]
    weight, moment, grad, orth, weight_out, moment_out, load_sem, store_sem = refs[36:]
    slots, base = weight.shape[0], weight.shape[1]
    arrays = ((QKV, 0), (QKV, 2), (QKV, 3), (OUT, 0), (GU, 0), (GU, 3), (DOWN, 0))
    tiles = []
    for matrix, (array, first) in enumerate(arrays):
        for row in range(weights[matrix].shape[0] // base):
            for column in range(weights[matrix].shape[1] // unit):
                tiles.append((matrix, array, row * base, column * unit, (first + column) * unit))

    def loads(t):
        matrix, array, row, column, array_column = tiles[t]
        here = (pl.ds(row, base), pl.ds(column, unit))
        there = (pl.ds(row, base), pl.ds(array_column, unit))
        slot = t % slots
        return [
            pltpu.make_async_copy(source, target.at[slot], load_sem.at[slot, k])
            for k, (source, target) in enumerate(
                (
                    (weights[matrix].at[here], weight), (moments[matrix].at[here], moment),
                    (sums[array].at[there], grad), (orths[array].at[there], orth),
                )
            )
        ]

    def stores(t):
        matrix, _, row, column, _ = tiles[t]
        here = (pl.ds(row, base), pl.ds(column, unit))
        slot = t % slots
        return [
            pltpu.make_async_copy(weight_out.at[slot], new_weights[matrix].at[here], store_sem.at[slot, 0]),
            pltpu.make_async_copy(moment_out.at[slot], new_moments[matrix].at[here], store_sem.at[slot, 1]),
        ]

    for t in range(slots - 1):
        for copy in loads(t):
            copy.start()
    few = 16
    for t in range(len(tiles)):
        slot = t % slots
        if t + slots - 1 < len(tiles):
            for copy in loads(t + slots - 1):
                copy.start()
        for copy in loads(t):
            copy.wait()
        if t >= slots:
            for copy in stores(t - slots):
                copy.wait()

        def act(k, carry):
            rows = pl.ds(pl.multiple_of(k * few, few), few)
            weight_out[slot, rows, :] = weight[slot, rows, :] * (
                1.0 - LEARN_RATE * WEIGHT_DECAY
            ) - LEARN_RATE * orth[slot, rows, :].astype(F32)
            moment_out[slot, rows, :] = MOMENTUM * moment[slot, rows, :] + grad[
                slot, rows, :
            ].astype(F32)
            return carry

        lax.fori_loop(0, base // few, act, 0)
        for copy in stores(t):
            copy.start()
    for t in range(len(tiles) - slots, len(tiles)):
        for copy in stores(t):
            copy.wait()


def apply_all(weights, moments, sums, orths, n, unit):
    slots, base = 4, unit // n
    dma = pltpu.SemaphoreType.DMA
    vmem = pltpu.VMEM
    results = pl.pallas_call(
        functools.partial(apply_kernel, unit),
        out_shape=[jax.ShapeDtypeStruct(matrix.shape, F32) for matrix in weights] * 2,
        in_specs=[ANY] * 22,
        out_specs=[ANY] * 14,
        scratch_shapes=[
            vmem((slots, base, unit), F32),
            vmem((slots, base, unit), F32),
            vmem((slots, base, unit), BF16),
            vmem((slots, base, unit), BF16),
            vmem((slots, base, unit), F32),
            vmem((slots, base, unit), F32),
            dma((slots, 4)),
            dma((slots, 2)),
        ],
        compiler_params=pltpu.CompilerParams(vmem_limit_bytes=56 * 2**20),
    )(*weights, *moments, *sums, *orths)
    return results[:7], results[7:]


def body(
    layer_input,
    output_grad,
    lengths,
    attention_gain,
    feed_gain,
    query_gain,
    key_gain,
    query_weight,
    key_weight,
    value_weight,
    out_weight,
    gate_weight,
    up_weight,
    down_weight,
    query_moment,
    key_moment,
    value_moment,
    out_moment,
    gate_moment,
    up_moment,
    down_moment,
):
    owned = (
        query_weight, key_weight, value_weight, out_weight, gate_weight, up_weight, down_weight,
    )
    moments = (
        query_moment, key_moment, value_moment, out_moment, gate_moment, up_moment, down_moment,
    )
    n = lax.axis_size("own")
    unit = layer_input.shape[1]
    core = lax.axis_index("rep") % 2

    def halves(*matrices):
        parts = []
        for matrix in matrices:
            width = matrix.shape[1] // 2
            parts.append(lax.dynamic_slice_in_dim(matrix, core * width, width, 1))
        return jnp.concatenate(parts, 1).astype(BF16)

    step = unit // 2
    gate_half, up_half = halves(gate_weight), halves(up_weight)
    shards = (
        halves(query_weight, key_weight, value_weight),
        out_weight.astype(BF16),
        jnp.concatenate(
            [part[:, k * step : (k + 1) * step] for k in range(3) for part in (gate_half, up_half)], 1
        ),
        down_weight.astype(BF16),
    )
    row_count = layer_input.shape[0]
    _, positions = segments(lengths[0], row_count)
    cosine_table, sine_table = rope_tables(positions)
    starts = (jnp.arange(row_count, dtype=jnp.int32) - positions).astype(F32)
    table = jnp.concatenate(
        [
            cosine_table[:, 0], cosine_table[:, 0], -sine_table[:, 0], sine_table[:, 0],
            jnp.broadcast_to(starts[:, None], (row_count, HEAD_DIM)),
        ],
        1,
    )
    gain_rows = [gain[None, :] for gain in (attention_gain, feed_gain, query_gain, key_gain)]
    (block_output, input_grad), gain_grads, grads = layer_pass(
        layer_input, output_grad, table, gain_rows, shards, n
    )
    gains = jnp.concatenate([grad[0] for grad in gain_grads])
    gains = jnp.pad(gains, (0, 24 * 128 - gains.shape[0])).reshape(24, 128)
    reduced, orth, gain_sums = update_all(grads, moments, gains, n, unit)
    new_weights, moments_next = apply_all(owned, moments, reduced, orth, n, unit)
    gain_sums = gain_sums.reshape(-1)
    norm_grads = gain_sums[: 2 * unit].reshape(2, unit)
    head_grads = gain_sums[2 * unit : 2 * unit + 2 * HEAD_DIM].reshape(2, HEAD_DIM)
    return (block_output, input_grad, norm_grads, head_grads, *new_weights, *moments_next)


def solution(mesh):
    tokens, owned = P(("rep", "own"), None), P("own", None)
    return jax.shard_map(
        body,
        mesh=mesh,
        in_specs=(tokens,) * 3 + (P(),) * 4 + (owned,) * 14,
        out_specs=(tokens,) * 2 + (P(),) * 2 + (owned,) * 14,
        check_vma=False,
    )
```

profile of v0, /device:TPU:15, one launch (start us, length us, event | category | flops | bytes accessed | tf_op | source)
XLA Modules:
  0.0 519.4 jit_solution(3062786337817544320)
XLA Ops:
  0.7 0.8 reduce-window.4
  1.5 0.7 fusion.3
  2.2 0.1 convert_reduce_fusion
  2.3 0.1 select_reduce_fusion
  2.4 0.1 broadcast_in_dim.42
  2.5 1.1 dynamic-slice_convert_fusion.2
  3.5 0.0 copy-start.1
  3.6 1.2 dynamic-slice_convert_fusion.3
  4.7 0.8 pad_maximum_fusion.refs_7_
  5.6 0.5 multiply_sine_fusion
  6.1 0.9 concatenate.13.refs_2_
  7.0 0.0 copy-done.1
  7.0 0.9 convert_element_type.35.refs_8_
  7.9 0.0 copy-start
  7.9 1.6 dynamic-slice_convert_fusion
  9.5 0.2 copy-done
  9.7 0.0 copy-start.2
  9.7 1.1 convert_element_type.38.refs_10_
  10.9 0.0 copy-done.2
  10.9 183.7 %shard_map.340 = (f32[256,1024]{1,0:T(8,128)}, f32[256,1024]{1,0:T(8,128)}, f32[1,1024]{1,0:T(1,128)}, f32[1,1024]{1,0:T(1,128)}, f32[1,128]{1,0:T(1,128)}, /*in...) custom-call(f32[256,1024]{1,0:T(8,128)} %refs_0_.2, ...), custom_call_target="tpu_custom_call" | custom-call | tf_op jit(solution)/shard_map/pallas_call | solution.py:532
  194.6 1.3 fusion.1.refs_11_
  195.9 304.1 %shard_map.341 = (bf16[128,4096]{1,0:T(8,128)(2,1)}, bf16[256,1024]{1,0:T(8,128)(2,1)}, bf16[128,6144]{1,0:T(8,128)(2,1)}, bf16[384,1024]{1,0:T(8,128)(2,1)}, bf...) custom-call(bf16[1024,2048]{1,0:T(8,128)(2,1)} %get-tuple-element.53, ...), custom_call_target="tpu_custom_call" | custom-call | tf_op jit(solution)/shard_map/pallas_call | solution.py:1408
  500.1 1.2 slice.33
  501.3 0.7 slice.32
  502.0 0.6 reshape.85
  502.6 0.0 copy-start.4
  502.6 14.2 %shard_map.342 = (f32[128,2048]{1,0:T(8,128)}, f32[128,1024]{1,0:T(8,128)}, f32[128,1024]{1,0:T(8,128)}, f32[256,1024]{1,0:T(8,128)}, f32[128,3072]{1,0:T(8,128)...) custom-call(f32[128,2048]{1,0:T(8,128)} %refs_0_.3, ...), custom_call_target="tpu_custom_call" | custom-call | tf_op jit(solution)/shard_map/pallas_call | solution.py:1526
  516.9 0.0 copy-start.3
  516.9 0.0 copy-done.4
  516.9 1.0 copy.47
  517.9 0.6 copy-done.3
  518.5 1.0 copy.48
  (8 shorter events, 0.1 us)
Async XLA Ops:
  3.5 3.4 copy-start.1
  7.9 1.9 copy-start
  9.7 1.1 copy-start.2
  502.6 14.3 %copy-start.4 = (f32[256,1024]{1,0:T(8,128)S(1)}, f32[256,1024]{1,0:T(8,128)}, u32[]{:S(2)}) copy-start(f32[256,1024]{1,0:T(8,128)} %get-tuple-element.111) | copy-start | bytes 3145732
  516.9 1.6 copy-start.3
where the time goes:
time: 520 us; the launch traced here: 519 us
  Pallas kernels  502 us (97%)
  local copies, waits for them, and re-layouts  10.2 us (2%)
  other arithmetic  6.33 us (1%)
    pallas_call x1, Pallas kernels, update_all(): pl.pallas_call(functools.partial(update_kernel, n, unit), out_shape=own +...  304 us
    pallas_call x1, Pallas kernels, layer_pass(): pl.pallas_call(functools.partial(layer_kernel, n, tokens, unit), out_shap...  184 us
    pallas_call x1, Pallas kernels, apply_all(): pl.pallas_call(functools.partial(apply_kernel, unit), out_shape=[jax.Shap...  14.2 us

commit v1 on v0

--- a/solution.py
+++ b/solution.py
@@ -120,11 +120,12 @@
     output, input_grad, grad_attention, grad_feed, grad_query_gain, grad_key_gain = refs[11:17]
     grads = refs[17:21]
     (
-        w_qkv, w_out, w_gu, w_down, normed, raw, low, probs, context, hidden, out_low, attended,
-        grad_context, activated, gu_back, part, sent, got, middle, tables, stage, turned_left, gain_sums,
+        w_qkv, w_out, w_gu, w_down, normed, raw, low, probs, context, hidden, out_low, activated, gu_back, part, sent, got, middle, tables, stage, turned_left, normed_turned, context_turned, hidden_turned,
+        gain_sums,
         local, ring_send, ring_recv, x_send, x_recv, swap_send, swap_recv, stage_sem,
     ) = refs[21:]
     weights = (w_qkv, w_out, w_gu, w_down)
+    grad_context, attended = normed, context
     place = Place(n)
     top = n // 2
     cw, ccw = place.ring_neighbour(1), place.ring_neighbour(-1)
@@ -265,12 +266,19 @@
         own = part[pl.ds(pl.multiple_of(mine + k, few), few), :]
         return own + got[slot, pl.ds(k, few), :].astype(F32)
 
-    def weight_grad(which, left, right):
+    def turn(left, target):
+        def act(k):
+            target[pl.ds(k, chunk), :] = left[:, pl.ds(k, chunk)].T
+
+        loop(left.shape[1], chunk, act)
+
+    def weight_grad(which, left, right, turned):
         columns = right.shape[1] // unit
 
         def by_rows(r, carry):
             row = pl.multiple_of(r * chunk, chunk)
-            turned_left[...] = left[:, pl.ds(row, chunk)].T
+            if turned is None:
+                turned_left[...] = left[:, pl.ds(row, chunk)].T
 
             def by_columns(c, carry):
                 column = pl.multiple_of(c * unit, unit)
@@ -281,7 +289,8 @@
                 def _():
                     stage_copy(which, slot, row, column, chunk, unit).wait()
 
-                value = dot(turned_left[...], right[:, pl.ds(column, unit)], NN)
+                block = turned_left[...] if turned is None else turned[pl.ds(row, chunk), :]
+                value = dot(block, right[:, pl.ds(column, unit)], NN)
                 stage[slot] = value.astype(BF16)
                 stage_copy(which, slot, row, column, chunk, unit).start()
                 return carry
@@ -337,6 +346,7 @@
     raw[:, pl.ds(unit, chunk)] = keys_values[:, :chunk]
     low[:, pl.ds(unit + chunk, chunk)] = keys_values[:, chunk:].astype(BF16)
     serve(*pending.pop(0))
+    turn(normed, normed_turned)
 
     def turned(value, rows):
         return value * tables[rows, pl.ds(0, HEAD_DIM)] + pltpu.roll(
@@ -398,6 +408,7 @@
     while pending and pending[0][0] == 1:
         serve(*pending.pop(0))
     partial_product(3, 0, context, w_out, NN)
+    turn(context, context_turned)
     if pending and pending[0][0] == 2:
         serve(*pending.pop(0))
     part_swap(3, 0).wait_recv()
@@ -408,10 +419,13 @@
     loop(tokens, few, add_middle)
     normalize(middle, feed_gain, hidden)
     rows_swap(4, hidden).start()
+    if pending:
+        serve(*pending.pop(0))
+    rows_swap(4, hidden).wait_recv()
+    turn(hidden, hidden_turned)
     while pending:
         serve(*pending.pop(0))
     take_x(2)
-    rows_swap(4, hidden).wait_recv()
     rows_swap(2, out_low).wait_recv()
 
     def feed(k):
@@ -431,7 +445,7 @@
     loop(ff, chunk, feed)
     part_swap(3, 0).wait_send()
     partial_product(6, 0, gu_back, w_gu, NT)
-    weight_grad(3, activated, out_low)
+    weight_grad(3, activated, out_low, None)
     part_swap(6, 0).wait_recv()
 
     def middle_back(k):
@@ -444,7 +458,7 @@
     loop(tokens, few, middle_back)
     rows_swap(7, attended).start()
     partial_product(5, 1, activated, w_down, NN)
-    weight_grad(2, hidden, gu_back)
+    weight_grad(2, hidden, gu_back, hidden_turned)
     part_swap(5, 1).wait_recv()
 
     def add_output(k):
@@ -453,8 +467,9 @@
     loop(tokens, few, add_output)
     rows_swap(7, attended).wait_recv()
 
+    rows_swap(0, normed).wait_send()
     grad_context[...] = dot(attended[...], w_out[...], NT).astype(BF16)
-    weight_grad(1, context, attended)
+    weight_grad(1, context, attended, context_turned)
 
     def head_back(rows, columns, gain, grad, index):
         value = raw[rows, columns]
@@ -493,7 +508,7 @@
 
     part_swap(6, 0).wait_send()
     partial_product(8, 0, low, w_qkv, NT)
-    weight_grad(0, normed, low)
+    weight_grad(0, normed, low, normed_turned)
     part_swap(8, 0).wait_recv()
 
     def input_back(k):
@@ -507,7 +522,7 @@
     grad_query_gain[...] = jnp.sum(gain_sums[2, :, pl.ds(0, HEAD_DIM)], 0, keepdims=True)
     grad_key_gain[...] = jnp.sum(gain_sums[3, :, pl.ds(0, HEAD_DIM)], 0, keepdims=True)
 
-    for index, ref in ((0, normed), (1, tables), (2, out_low), (4, hidden), (7, attended)):
+    for index, ref in ((1, tables), (2, out_low), (4, hidden), (7, attended)):
         rows_swap(index, ref).wait_send()
     part_swap(5, 1).wait_send()
     part_swap(8, 0).wait_send()
@@ -545,8 +560,6 @@
             vmem((both, unit), BF16),
             vmem((both, unit), BF16),
             vmem((both, unit), BF16),
-            vmem((both, unit), BF16),
-            vmem((both, unit), BF16),
             vmem((both, 3 * unit // 2), BF16),
             vmem((both, 3 * unit), BF16),
             vmem((both, unit), F32),
@@ -556,6 +569,9 @@
             vmem((both, 3 * HEAD_DIM), F32),
             vmem((2, unit // 2, unit), BF16),
             vmem((unit // 2, both), BF16),
+            vmem((unit, both), BF16),
+            vmem((unit, both), BF16),
+            vmem((unit, both), BF16),
             vmem((4, 8, unit), F32),
             dma((4,)),
             dma((8 * top,)),
@@ -587,8 +603,8 @@
 KEY, VALUE, QUERY, OUTM, GATE, UP, DOWNM = range(7)
 RETURNS = (OUTM, KEY, VALUE, DOWNM, GATE, UP, QUERY)
 TILE_SLOTS = 4
-X_AHEAD = 4
-LAND_AHEAD = 6
+X_AHEAD = 8
+LAND_AHEAD = 16
 
 
 def summing_core(phase):
@@ -1109,7 +1125,7 @@
             if summing_core(phase) == core:
                 load_moment(phase)
         done, sent, hop = 0, 0, 0
-        for index in range(LAND_AHEAD):
+        for index in range(min(LAND_AHEAD, len(landed))):
             land_copy(*landed[index][1:], "start")
         for index in range(TILE_SLOTS - 1):
             prefetch(rings, index)

time: 520 us -> 519 us (level)
  no operation moved by 1% of the time
where the time goes in v1:
time: 519 us
  Pallas kernels  501 us (97%)
  local copies, waits for them, and re-layouts  10.2 us (2%)
  other arithmetic  6.33 us (1%)
    pallas_call x1, Pallas kernels, update_all(): pl.pallas_call(functools.partial(update_kernel, n, unit), out_shape=own +...  304 us
    pallas_call x1, Pallas kernels, layer_pass(): pl.pallas_call(functools.partial(layer_kernel, n, tokens, unit), out_shap...  183 us
    pallas_call x1, Pallas kernels, apply_all(): pl.pallas_call(functools.partial(apply_kernel, unit), out_shape=[jax.Shap...  14.2 us

profile of v1, /device:TPU:15, one launch (start us, length us, event | category | flops | bytes accessed | tf_op | source)
XLA Modules:
  0.0 518.5 jit_solution(11121538319744566592)
XLA Ops:
  0.7 0.8 reduce-window.4
  1.5 0.7 fusion.3
  2.2 0.1 convert_reduce_fusion
  2.3 0.1 select_reduce_fusion
  2.4 0.1 broadcast_in_dim.42
  2.5 1.1 dynamic-slice_convert_fusion.2
  3.5 0.0 copy-start.1
  3.6 1.2 dynamic-slice_convert_fusion.3
  4.7 0.8 pad_maximum_fusion.refs_7_
  5.6 0.5 multiply_sine_fusion
  6.1 0.9 concatenate.13.refs_2_
  7.0 0.0 copy-done.1
  7.0 0.9 convert_element_type.35.refs_8_
  7.9 0.0 copy-start
  7.9 1.6 dynamic-slice_convert_fusion
  9.5 0.2 copy-done
  9.7 0.0 copy-start.2
  9.7 1.1 convert_element_type.38.refs_10_
  10.9 0.0 copy-done.2
  10.9 182.8 %shard_map.340 = (f32[256,1024]{1,0:T(8,128)}, f32[256,1024]{1,0:T(8,128)}, f32[1,1024]{1,0:T(1,128)}, f32[1,1024]{1,0:T(1,128)}, f32[1,128]{1,0:T(1,128)}, /*in...) custom-call(f32[256,1024]{1,0:T(8,128)} %refs_0_.2, ...), custom_call_target="tpu_custom_call" | custom-call | tf_op jit(solution)/shard_map/pallas_call | solution.py:547
  193.7 1.3 fusion.1.refs_11_
  195.0 304.1 %shard_map.341 = (bf16[128,4096]{1,0:T(8,128)(2,1)}, bf16[256,1024]{1,0:T(8,128)(2,1)}, bf16[128,6144]{1,0:T(8,128)(2,1)}, bf16[384,1024]{1,0:T(8,128)(2,1)}, bf...) custom-call(bf16[1024,2048]{1,0:T(8,128)(2,1)} %get-tuple-element.53, ...), custom_call_target="tpu_custom_call" | custom-call | tf_op jit(solution)/shard_map/pallas_call | solution.py:1424
  499.1 1.2 slice.33
  500.4 0.7 slice.32
  501.1 0.6 reshape.85
  501.7 0.0 copy-start.4
  501.7 14.2 %shard_map.342 = (f32[128,2048]{1,0:T(8,128)}, f32[128,1024]{1,0:T(8,128)}, f32[128,1024]{1,0:T(8,128)}, f32[256,1024]{1,0:T(8,128)}, f32[128,3072]{1,0:T(8,128)...) custom-call(f32[128,2048]{1,0:T(8,128)} %refs_0_.3, ...), custom_call_target="tpu_custom_call" | custom-call | tf_op jit(solution)/shard_map/pallas_call | solution.py:1542
  515.9 0.0 copy-start.3
  515.9 0.0 copy-done.4
  516.0 1.0 copy.47
  516.9 0.6 copy-done.3
  517.5 1.0 copy.48
  (8 shorter events, 0.1 us)
Async XLA Ops:
  3.5 3.4 copy-start.1
  7.9 1.9 copy-start
  9.7 1.1 copy-start.2
  501.7 14.3 %copy-start.4 = (f32[256,1024]{1,0:T(8,128)S(1)}, f32[256,1024]{1,0:T(8,128)}, u32[]{:S(2)}) copy-start(f32[256,1024]{1,0:T(8,128)} %get-tuple-element.111) | copy-start | bytes 3145732
  515.9 1.6 copy-start.3
